TPU v7x, 256 devices: a whole 4x4x8 slice. The times are simulated.
256 devices in a mesh: row: 16 (over z, y_lo), col: 8 (over x, core), rep: 2 (over y_hi).
Axes of the slice: x: 4, y: 4 (y_hi: 2, y_lo: 2; y = y_hi * 2 + y_lo), z: 8, core: 2. Of those that a mesh axis runs over, the one named last changes fastest.
Arguments:
- a_blocks: bfloat16 [128, 16, 2, 128, 128], P('row', 'col'), may hold values from -0.25 to 0.25
- a_index: int32 [128, 16, 2], P('row', 'col'), may hold values from 0 to 63, as said below
- a_count: int32 [128, 16], P('row', 'col'), may hold values from 0 to 2, as said below
- b_blocks: bfloat16 [16, 8, 32, 128, 128], P('row', 'col'), may hold values from -6 to 6
- b_rows: int32 [16, 8, 32], P('row', 'col'), may hold values from 0 to 63, as said below
- b_cols: int32 [16, 8, 32], P('row', 'col'), may hold values from 0 to 63
- b_count: int32 [16, 8], P('row', 'col'), may hold values from 16 to 32, as said below
- c_cols: int32 [128, 8, 4], P('row', 'col'), may hold values from 0 to 63, as said below
- c_count: int32 [128, 8], P('row', 'col'), may hold values from 1 to 4, as said below
Outputs:
- c_blocks: bfloat16 [128, 8, 4, 128, 128], P(('row', 'rep'), 'col')
Inputs may be any that keep to these rules, and one draw needn't show every extreme that they name: Live slots come first: slot a of block row i in piece p is live when a < a_count[i, p]. `a_index`: the slots of one block row and piece name distinct block rows of that piece. Live slots come first: slot m of list (p, q) is live when m < b_count[p, q]. `b_rows`: the slots of one list name distinct block rows of the piece. Live slots come first: slot s of block row i in group q is live when s < c_count[i, q]. `c_cols`: the slots of one block row and group name distinct block columns.
All inputs are finite; a program needn't handle non-finite values.
Results may differ from a plain program's by a relative error of at most 0.001.
Values may be sent and summed in bfloat16 or wider, within the bound.
No kernel may reach another device: no remote copies, remote signals or barrier semaphores. Data moves between devices by JAX's collectives and lax.ppermute only.
A program may use at most 64 MiB of HBM per device.

v0:
```python
import functools

import jax
import jax.numpy as jnp
from jax import lax
from jax.experimental import pallas as pl
from jax.experimental.pallas import tpu as pltpu
from jax.sharding import Mesh
from jax.sharding import PartitionSpec as P

NZ, NYL, NX, NCORE, NREP = 8, 2, 4, 2, 2
AXES = ("z", "yl", "x", "core", "rep")
COL = ("x", "core")
BS, SA, SC, MB = 128, 2, 4, 32
ROWS = 4
PAIR = ROWS * 2 * SA
CAP = 8
HDR = 16
LANES = 128
SHIFTS = (0, 4, 3, -3, 2, -2, 1, -1)
FAR = 5
EARLY = 4


def along_y(value, steps, other_core):
    n = NYL * NREP
    pairs = []
    for y in range(n):
        for core in range(NCORE):
            ends = []
            for where, at in ((y, core), ((y + steps) % n, core ^ other_core)):
                ends.append(((where % NYL) * NCORE + at) * NREP + where // NYL)
            pairs.append(tuple(ends))
    return lax.ppermute(value, ("yl", "core", "rep"), pairs)


def shift_z(value, steps):
    if steps == 0:
        return value
    return lax.ppermute(value, "z", [(z, (z + steps) % NZ) for z in range(NZ)])


def swap(value):
    return lax.ppermute(value, "core", [(0, 1), (1, 0)])


def find_codes(wanted, columns, own, other, is_own, lane):
    slot = jnp.zeros((NZ, LANES), jnp.int32)
    target = jnp.full((NZ, LANES), -5, jnp.int32)
    for m in range(MB):
        hit = wanted == jnp.where(is_own, own[0, m], other[0, m])
        slot = jnp.where(hit, m, slot)
        target = jnp.where(hit, jnp.where(is_own, own[1, m], other[1, m]), target)
    moved = {d: pltpu.roll(columns, d % LANES, 1) if d else columns for d in range(1 - SC, SC)}
    code = jnp.full((NZ, LANES), -1, jnp.int32)
    for s in range(SC):
        column = moved[-s]
        for o in range(1, SC):
            column = jnp.where((lane & (SC - 1)) == o, moved[o - s], column)
        code = jnp.where(column == target, slot * SC + s, code)
    return code


def pack_kernel(shifts, lo, size, meta, own, other, twin_other, *rest):
    lists, outs = rest[:4], rest[4 : 4 + len(shifts)]
    held, codes, scalars, sems = rest[4 + len(shifts) :]
    core = lax.axis_index("core")
    mine, twins = core * 2 * MB, (1 - core) * 2 * MB
    copies = []
    for n, (source, first) in enumerate(zip(lists, (mine, mine + MB, twins, twins + MB))):
        copies.append(pltpu.make_async_copy(source, held.at[pl.ds(first, MB)], sems.at[n]))
        copies[-1].start()
    yl = lax.axis_index("yl")
    me = lax.axis_index("z")
    x = lax.axis_index("x")
    lane = lax.broadcasted_iota(jnp.int32, (NZ, LANES), 1)
    is_own = ((lane >> 1) & 1) == yl
    first_half = lax.axis_index("rep") == 0

    def pick(col, start, length):
        rows = jnp.concatenate([meta[z, pl.ds(col, 1), :] for z in range(NZ)], axis=0)
        low = pltpu.roll(rows, LANES - start, 1) if start else rows
        return jnp.where(first_half, low, pltpu.roll(rows, LANES - start - length, 1))

    wanted = jnp.where(lane < PAIR, pick(me, 0, PAIR), -2)
    twin_meta = meta[me, pl.ds(x * NCORE + 1 - core, 1), :]
    twin_own = {
        (n, m): twin_meta[:, 4 * PAIR + n * MB + m : 4 * PAIR + n * MB + m + 1] for n in range(2) for m in range(MB)
    }
    code = find_codes(wanted, pick(x * NCORE + core, 2 * PAIR, ROWS * SC), own, other, is_own, lane)
    twin = find_codes(wanted, pick(x * NCORE + 1 - core, 2 * PAIR, ROWS * SC), twin_own, twin_other, is_own, lane)
    code, twin = jnp.where(core == 0, code, twin), jnp.where(core == 0, twin, code)
    code = jnp.where(lane < PAIR, code, jnp.where(lane < 2 * PAIR, pltpu.roll(twin, PAIR, 1), -1))
    codes[...] = code
    to_scalars = pltpu.make_async_copy(codes, scalars, sems.at[4])
    to_scalars.start()
    head = jnp.concatenate([code, jnp.full((HDR - NZ, LANES), -1, jnp.int32)], axis=0)
    head = head.astype(jnp.float32).astype(jnp.bfloat16)
    for out, shift in zip(outs, shifts):
        out[pl.ds((size if shift else PAIR) * BS, HDR), :] = head
    to_scalars.wait()
    for copy in copies:
        copy.wait()

    def block(t, code):
        return (t >> 4) * (2 * MB) + jnp.where(((t >> 1) & 1) == yl, 0, MB) + (code >> 2)

    for out, shift in zip(outs, shifts):
        z = lax.rem(me + (NZ + shift), NZ)

        def step(t, count, out=out, z=z):
            code = scalars[z, t]
            hit = code >= 0
            place = count >> 1

            @pl.when(hit & ((count & 1) == core) & (place >= lo) & (place < lo + size))
            def _():
                out[pl.ds(pl.multiple_of((place - lo) * BS, BS), BS), :] = held[block(t, code)]

            return count + hit.astype(jnp.int32)

        def steps(n, count, step=step):
            for k in range(8):
                count = step(n * 8 + k, count)
            return count

        def own_step(t, count, out=out, z=z):
            t = core * PAIR + t
            code = scalars[z, t]
            hit = code >= 0

            @pl.when(hit)
            def _():
                out[pl.ds(pl.multiple_of(count * BS, BS), BS), :] = held[block(t, code)]

            return count + hit.astype(jnp.int32)

        if shift:
            lax.fori_loop(0, 2 * PAIR // 8, steps, jnp.int32(0))
        else:
            lax.fori_loop(0, PAIR, own_step, jnp.int32(0))


def pack(meta, lists, blocks, shifts, lo, size):
    smem, vmem, hbm = (pl.BlockSpec(memory_space=m) for m in (pltpu.SMEM, pltpu.VMEM, pl.ANY))
    return pl.pallas_call(
        functools.partial(pack_kernel, shifts, lo, size),
        out_shape=[
            jax.ShapeDtypeStruct(((size if shift else PAIR) * BS + HDR, BS), jnp.bfloat16)
            for shift in shifts
        ],
        in_specs=[vmem] + [smem] * 3 + [hbm] * 4,
        out_specs=[vmem] * len(shifts),
        scratch_shapes=[
            pltpu.VMEM((4 * MB, BS, BS), jnp.bfloat16),
            pltpu.VMEM((NZ, LANES), jnp.int32),
            pltpu.SMEM((NZ, LANES), jnp.int32),
            pltpu.SemaphoreType.DMA((5,)),
        ],
        compiler_params=pltpu.CompilerParams(vmem_limit_bytes=28 * 2**20),
        name="pack",
    )(meta, *lists, *blocks)


def consume_kernel(shifts, parts, a_all, own_in, twin_in, longest_in, *rest):
    width = {shift: len(parts) if shift else 1 for shift in shifts}
    count_msgs = sum(width.values())
    msgs, (own_out, twin_out, longest, totals, codes, scalars, sem) = rest[:count_msgs], rest[count_msgs:]
    n_sums = ROWS * SC
    groups = {}
    for shift in shifts:
        groups[shift], msgs = msgs[: width[shift]], msgs[width[shift] :]
    me = lax.axis_index("z")
    core = lax.axis_index("core")
    row = lax.broadcasted_iota(jnp.int32, (HDR, LANES), 0)
    most = jnp.zeros((HDR, 1), jnp.int32)
    for n, shift in enumerate(shifts):
        source = lax.rem(me + (NZ - shift), NZ)
        head = groups[shift][0][pl.ds((parts[0][1] if shift else PAIR) * BS, HDR), :]
        head = head.astype(jnp.float32).astype(jnp.int32)
        codes[pl.ds(n, 1), :] = jnp.sum(jnp.where(row == me, head, 0), axis=0, keepdims=True)
        sent = (head >= 0) & (row != source)
        most = jnp.maximum(most, jnp.sum(sent.astype(jnp.int32), axis=1, keepdims=True))
    to_scalars = pltpu.make_async_copy(codes, scalars, sem)
    to_scalars.start()
    most = jnp.broadcast_to(jnp.max(most, axis=0, keepdims=True), longest.shape)
    longest[...] = jnp.maximum(most, longest_in[...])
    totals[:n_sums] = own_in[...]
    totals[n_sums:] = twin_in[...]
    to_scalars.wait()

    def add(wanted, whose, source, t, code, msg, place):
        @pl.when(wanted)
        def _():
            block = msg[pl.ds(pl.multiple_of(place * BS, BS), BS), :]
            target = whose * n_sums + (t >> 2) * SC + (code & 3)
            totals[target] += jnp.dot(a_all[source, t], block, preferred_element_type=jnp.float32)

    for n, shift in enumerate(shifts):
        source = lax.rem(me + (NZ - shift), NZ)
        group = groups[shift]

        def step(t, count, n=n, source=source, group=group):
            code = scalars[n, t]
            hit = code >= 0
            place = count >> 1
            whose = (t >> 4) ^ core
            for (lo, size), msg in zip(parts, group):
                here = hit & ((count & 1) == core) & (place >= lo) & (place < lo + size)
                add(here, whose, source, t & (PAIR - 1), code, msg, place - lo)
            return count + hit.astype(jnp.int32)

        def own_step(t, count, n=n, source=source, group=group):
            code = scalars[n, core * PAIR + t]
            hit = code >= 0
            add(hit, 0, source, t, code, group[0], count)
            return count + hit.astype(jnp.int32)

        if shift:
            lax.fori_loop(0, 2 * PAIR, step, jnp.int32(0))
        else:
            lax.fori_loop(0, PAIR, own_step, jnp.int32(0))
    own_out[...] = totals[:n_sums]
    twin_out[...] = totals[n_sums:]


def consume(a_all, sums, longest, shifts, parts, msgs):
    vmem = pl.BlockSpec(memory_space=pltpu.VMEM)
    return pl.pallas_call(
        functools.partial(consume_kernel, shifts, parts),
        out_shape=(
            jax.ShapeDtypeStruct((ROWS * SC, BS, BS), jnp.float32),
            jax.ShapeDtypeStruct((ROWS * SC, BS, BS), jnp.float32),
            jax.ShapeDtypeStruct((8, LANES), jnp.int32),
        ),
        in_specs=[vmem] * (4 + len(msgs)),
        out_specs=(vmem, vmem, vmem),
        scratch_shapes=[
            pltpu.VMEM((2 * ROWS * SC, BS, BS), jnp.float32),
            pltpu.VMEM((NZ, LANES), jnp.int32),
            pltpu.SMEM((NZ, LANES), jnp.int32),
            pltpu.SemaphoreType.DMA,
        ],
        compiler_params=pltpu.CompilerParams(vmem_limit_bytes=28 * 2**20),
        cost_estimate=pl.CostEstimate(flops=2 * BS**3 * 40, bytes_accessed=8 * 2**20, transcendentals=0),
        name="consume",
    )(a_all, *sums, longest, *msgs)


def body(a_blocks, a_index, a_count, b_blocks, b_rows, b_cols, b_count, c_cols, c_count):
    rep = lax.axis_index("rep")
    a_all = lax.dynamic_slice_in_dim(a_blocks, rep * ROWS, ROWS, 0).reshape(PAIR, BS, BS)
    a_all = lax.all_gather(a_all, COL)

    slots_b = jnp.arange(MB, dtype=jnp.int32)
    own = jnp.stack([jnp.where(slots_b < b_count[0, 0], b_rows[0, 0], -1), b_cols[0, 0]])
    slots_a = jnp.arange(SA, dtype=jnp.int32)
    a_meta = jnp.where(slots_a < a_count[:, :, None], a_index, -2)
    slots_c = jnp.arange(SC, dtype=jnp.int32)
    c_meta = jnp.where(slots_c < c_count[:, :, None], c_cols, -1)
    b_own = b_blocks[0, 0]

    blocks = [b_own, along_y(b_own, 1, 0), swap(b_own), along_y(b_own, -1, 1)]
    lists = [own, along_y(own, 1, 0), along_y(own, -1, 1)]

    meta = jnp.concatenate([a_meta.reshape(2 * PAIR), c_meta.reshape(2 * ROWS * SC), own.reshape(2 * MB)])
    meta = jnp.broadcast_to(meta[None, :], (NZ * NX * NCORE, LANES))
    meta = lax.all_to_all(meta, ("z", "x", "core"), 0, 0).reshape(NZ, NX * NCORE, LANES)

    def send(shifts, lo, size):
        outs = pack(meta, lists, blocks, shifts, lo, size)
        return [shift_z(out, shift) for out, shift in zip(outs, shifts)]

    def finish(own_sums, twin_sums):
        return (own_sums + twin_sums).astype(jnp.bfloat16)

    first = (0, CAP)
    msgs = send(SHIFTS[1:FAR], *first)
    near = send(SHIFTS[FAR:] + SHIFTS[:1], *first)
    msgs = near[-1:] + msgs + near[:-1]
    zero = [jnp.zeros((ROWS * SC, BS, BS), jnp.float32)] * 2
    longest = jnp.zeros((8, LANES), jnp.int32)
    *sums, longest = consume(a_all, zero, longest, SHIFTS[:EARLY], [first], msgs[:EARLY])
    *sums, longest = consume(a_all, sums, longest, SHIFTS[EARLY:], [first], msgs[EARLY:])

    def again(*_):
        rest = (CAP, PAIR - CAP)
        both = msgs[:1] + [m for pair in zip(msgs[1:], send(SHIFTS[1:], *rest)) for m in pair]
        own_sums, twin_sums, _ = consume(a_all, zero, longest, SHIFTS, [first, rest], both)
        return finish(own_sums, swap(twin_sums))

    out = lax.cond(longest[0, 0] > 2 * CAP, again, finish, sums[0], swap(sums[1]))
    return out.reshape(ROWS, 1, SC, BS, BS)


def solution(mesh):
    fine = Mesh(mesh.devices.reshape(NZ, NYL, NX, NCORE, NREP), AXES)
    row = ("z", "yl")
    return jax.shard_map(
        body,
        mesh=fine,
        in_specs=tuple(
            P(row, COL, *([None] * (rank - 2))) for rank in (5, 3, 2, 5, 3, 3, 2, 3, 2)
        ),
        out_specs=P(("z", "yl", "rep"), COL, None, None, None),
        check_vma=False,
    )
```

profile of v0, /device:TPU:1, one launch (start us, length us, event | category | flops | bytes accessed | tf_op | source)
XLA Modules:
  0.0 112.3 jit_solution(10567200147427040204)
XLA Ops:
  6.5 1.2 %copy-done = bf16[8,2,2,128,128]{4,3,2,1,0:T(8,128)(2,1)S(1)} copy-done((bf16[8,2,2,128,128]{4,3,2,1,0:T(8,128)(2,1)S(1)}, bf16[8,2,2,128,128]{4,3,2,1,0:T(8,128)(2,1)}, u32[]{:S(2)}) %copy-start) | copy-done | bytes 1048600
  7.8 0.8 constant_dynamic-slice_fusion
  8.6 0.0 all-gather.2.cloned.1.call-update
  8.6 4.2 %collective-permute-start.12 = (bf16[32,128,128]{2,1,0:T(8,128)(2,1)}, bf16[32,128,128]{2,1,0:T(8,128)(2,1)S(1)}, u32[]{:S(2)}, u32[]{:S(2)}) collective-permute-start(bf16[32,128,128]{2,1,0:T(8,128)(2,1)} %bitcast.18), channel_id=1, source_target_pairs={{0,19},{2,17},{16,2},{18,0},{1,18},{3,16},{17,3},{19,1},{4,23},{6,... | collective-permute-start | bytes 3145736 | tf_op jit(solution)/shard_map/ppermute | solution.py:34
  12.8 0.5 collective-permute-start.10
  14.0 0.7 compare_select_fusion.1
  14.6 0.7 pad_add_fusion.own
  15.3 0.1 reshape.88
  15.4 0.7 fusion
  16.0 0.1 copy.19
  16.1 0.1 reshape.87
  16.2 0.7 compare_select_fusion
  16.9 0.1 copy.18
  17.0 0.1 reshape.86
  17.1 0.1 pad_add_fusion.1
  17.2 0.6 broadcast_in_dim.36
  17.8 11.5 %all-to-all-start = ((s32[64,1,128]{2,1,0:T(1,128)}), s32[64,1,128]{2,1,0:T(1,128)S(1)}, u32[]{:S(2)}, u32[]{:S(2)}) async-start(s32[64,1,128]{2,1,0:T(1,128)} %broadcast_in_dim.36), calls=%async_computation | async-start | bytes 65536 | tf_op jit(solution)/shard_map/all_to_all | solution.py:268
  29.3 3.4 %collective-permute-start.9 = (s32[2,32]{1,0:T(2,128)S(1)}, s32[2,32]{1,0:T(2,128)S(1)}, u32[]{:S(2)}, u32[]{:S(2)}) collective-permute-start(s32[2,32]{1,0:T(2,128)S(1)} %pad_add_fusion.own), channel_id=1, source_target_pairs={{0,19},{2,17},{16,2},{18,0},{1,18},{3,16},{17,3},{19,1},{4,23},{6,... | collective-permute-start | bytes 776 | tf_op jit(solution)/shard_map/ppermute | solution.py:34
  32.7 0.0 collective-permute-start.8
  32.7 3.4 %collective-permute-done.9.twin_other = s32[2,32]{1,0:T(2,128)S(1)} collective-permute-done((s32[2,32]{1,0:T(2,128)S(1)}, s32[2,32]{1,0:T(2,128)S(1)}, u32[]{:S(2)}, u32[]{:S(2)}) %collective-permute-start.9) | collective-permute-done | bytes 288 | tf_op jit(solution)/shard_map/ppermute | solution.py:34
  36.1 2.5 %collective-permute-done.8.other = s32[2,32]{1,0:T(2,128)S(1)} collective-permute-done((s32[2,32]{1,0:T(2,128)S(1)}, s32[2,32]{1,0:T(2,128)S(1)}, u32[]{:S(2)}, u32[]{:S(2)}) %collective-permute-start.8) | collective-permute-done | bytes 288 | tf_op jit(solution)/shard_map/ppermute | solution.py:34
  38.6 0.1 all-to-all-done
  38.7 0.0 collective-permute-done.12.rest_3_
  38.7 0.0 collective-permute-done.11.rest_2_
  38.7 3.5 %pack.5 = (bf16[1040,128]{1,0:T(8,128)(2,1)S(1)}, bf16[1040,128]{1,0:T(8,128)(2,1)S(1)}, bf16[1040,128]{1,0:T(8,128)(2,1)S(1)}, bf16[1040,128]{1,0:T(8,128)(2,1)S(1)}) custom-call(s32[8,8,128]{2,1,0:T(8,128)S(1)} %bitcast.25, s32[2,32]{1,0:T(2,128)S(1)} %pad_add_fusion.own, s32[2,32]{1,0:T(2,128)S(1)} %collective-permute-done.8.other, ...), custom_call_target="tpu_custom_call" | custom-call | tf_op jit(solution)/shard_map/pack/pallas_call | solution.py:146
  42.3 7.1 %collective-permute-start.13 = (bf16[1040,128]{1,0:T(8,128)(2,1)S(1)}, bf16[1040,128]{1,0:T(8,128)(2,1)S(1)}, u32[]{:S(2)}, u32[]{:S(2)}) collective-permute-start(bf16[1040,128]{1,0:T(8,128)(2,1)S(1)} %get-tuple-element.93), channel_id=1, source_target_pairs={{0,128},{32,160},{64,192},{96,224},{128,0},{160,32},{192,64},{224,... | collective-permute-start | bytes 798728 | tf_op jit(solution)/shard_map/ppermute | solution.py:40
  49.4 2.0 %collective-permute-start.14 = (bf16[1040,128]{1,0:T(8,128)(2,1)S(1)}, bf16[1040,128]{1,0:T(8,128)(2,1)S(1)}, u32[]{:S(2)}, u32[]{:S(2)}) collective-permute-start(bf16[1040,128]{1,0:T(8,128)(2,1)S(1)} %get-tuple-element.94), channel_id=1, source_target_pairs={{0,96},{32,128},{64,160},{96,192},{128,224},{160,0},{192,32},{224,... | collective-permute-start | bytes 798728 | tf_op jit(solution)/shard_map/ppermute | solution.py:40
  51.3 2.5 %collective-permute-start.15 = (bf16[1040,128]{1,0:T(8,128)(2,1)S(1)}, bf16[1040,128]{1,0:T(8,128)(2,1)}, u32[]{:S(2)}, u32[]{:S(2)}) collective-permute-start(bf16[1040,128]{1,0:T(8,128)(2,1)S(1)} %get-tuple-element.95), channel_id=1, source_target_pairs={{0,160},{32,192},{64,224},{96,0},{128,32},{160,64},{192,96},{224,1... | collective-permute-start | bytes 798728 | tf_op jit(solution)/shard_map/ppermute | solution.py:40
  53.8 1.0 collective-permute-start.16
  54.8 4.7 %pack.4 = (bf16[1040,128]{1,0:T(8,128)(2,1)S(1)}, bf16[1040,128]{1,0:T(8,128)(2,1)S(1)}, bf16[1040,128]{1,0:T(8,128)(2,1)S(1)}, bf16[2064,128]{1,0:T(8,128)(2,1)}) custom-call(s32[8,8,128]{2,1,0:T(8,128)S(1)} %bitcast.26, s32[2,32]{1,0:T(2,128)S(1)} %pad_add_fusion.own, s32[2,32]{1,0:T(2,128)S(1)} %collective-permute-done.8.other, ...), custom_call_target="tpu_custom_call" | custom-call | tf_op jit(solution)/shard_map/pack/pallas_call | solution.py:146
  59.6 2.1 %collective-permute-start.17 = (bf16[1040,128]{1,0:T(8,128)(2,1)S(1)}, bf16[1040,128]{1,0:T(8,128)(2,1)}, u32[]{:S(2)}, u32[]{:S(2)}) collective-permute-start(bf16[1040,128]{1,0:T(8,128)(2,1)S(1)} %get-tuple-element.100), channel_id=1, source_target_pairs={{0,192},{32,224},{64,0},{96,32},{128,64},{160,96},{192,128},{224,1... | collective-permute-start | bytes 798728 | tf_op jit(solution)/shard_map/ppermute | solution.py:40
  61.7 1.0 collective-permute-start.18
  62.7 19.2 %collective-permute-done.14.rest_2_ = bf16[1040,128]{1,0:T(8,128)(2,1)S(1)} collective-permute-done((bf16[1040,128]{1,0:T(8,128)(2,1)S(1)}, bf16[1040,128]{1,0:T(8,128)(2,1)S(1)}, u32[]{:S(2)}, u32[]{:S(2)}) %collective-permute-start.14) | collective-permute-done | bytes 266272 | tf_op jit(solution)/shard_map/ppermute | solution.py:40
  81.9 0.0 collective-permute-start.19
  81.9 0.7 copy-done.8
  82.6 0.1 broadcast_in_dim.31.own_in.twin_in
  82.7 5.9 %consume.4 = (f32[16,128,128]{2,1,0:T(8,128)S(1)}, f32[16,128,128]{2,1,0:T(8,128)S(1)}, s32[8,128]{1,0:T(8,128)S(1)}) custom-call(bf16[8,16,128,128]{3,2,1,0:T(8,128)(2,1)} %all-gather.2.cloned.1.call-done.a_all, f32[16,128,128]{2,1,0:T(8,128)S(1)} %broadcast_in_dim.31.own_in.twin_in, f32[16,128,128]{2,1,0:T(8,128)S(1)} %broadcast_in_dim.31.own_in.twin_in, ...), custom_call_target="tpu_custom_call" | custom-call | flops 167772160 | bytes 8388608 | tf_op jit(solution)/shard_map/consume/pallas_call | solution.py:229
  88.7 1.4 %collective-permute-done.17.rest_1_ = bf16[1040,128]{1,0:T(8,128)(2,1)} collective-permute-done((bf16[1040,128]{1,0:T(8,128)(2,1)S(1)}, bf16[1040,128]{1,0:T(8,128)(2,1)}, u32[]{:S(2)}, u32[]{:S(2)}) %collective-permute-start.17) | collective-permute-done | bytes 266272 | tf_op jit(solution)/shard_map/ppermute | solution.py:40
  90.2 5.3 %collective-permute-done.18.rest_2_ = bf16[1040,128]{1,0:T(8,128)(2,1)} collective-permute-done((bf16[1040,128]{1,0:T(8,128)(2,1)S(1)}, bf16[1040,128]{1,0:T(8,128)(2,1)}, u32[]{:S(2)}, u32[]{:S(2)}) %collective-permute-start.18) | collective-permute-done | bytes 266272 | tf_op jit(solution)/shard_map/ppermute | solution.py:40
  95.5 0.3 collective-permute-done.19.rest_3_
  95.8 4.7 %consume.5 = (f32[16,128,128]{2,1,0:T(8,128)S(1)}, f32[16,128,128]{2,1,0:T(8,128)S(1)}, s32[8,128]{1,0:T(8,128)S(1)}) custom-call(bf16[8,16,128,128]{3,2,1,0:T(8,128)(2,1)S(1)} %copy-done.1, f32[16,128,128]{2,1,0:T(8,128)S(1)} %get-tuple-element.96.own_in, f32[16,128,128]{2,1,0:T(8,128)S(1)} %get-tuple-element.97.twin_in, ...), custom_call_target="tpu_custom_call" | custom-call | flops 167772160 | bytes 8388608 | tf_op jit(solution)/shard_map/consume/pallas_call | solution.py:229
  100.6 1.6 %collective-permute-start.20 = (f32[16,128,128]{2,1,0:T(8,128)S(1)}, f32[16,128,128]{2,1,0:T(8,128)S(1)}, u32[]{:S(2)}, u32[]{:S(2)}) collective-permute-start(f32[16,128,128]{2,1,0:T(8,128)S(1)} %get-tuple-element.105), channel_id=1, source_target_pairs={{0,2},{2,0},{1,3},{3,1},{4,6},{6,4},{5,7},{7,5},{8,10},{10,8},{9,1... | collective-permute-start | bytes 3145736 | tf_op jit(solution)/shard_map/ppermute | solution.py:44
  102.2 0.5 slice.3
  103.3 1.1 collective-permute-done.20
  104.5 0.1 conditional.1
  104.5 0.1 add_convert_fusion
  104.6 0.0 copy-start.10
  104.6 0.8 copy-done.10
  (26 shorter events, 0.1 us)
Async XLA Ops:
  6.5 1.2 %copy-start = (bf16[8,2,2,128,128]{4,3,2,1,0:T(8,128)(2,1)S(1)}, bf16[8,2,2,128,128]{4,3,2,1,0:T(8,128)(2,1)}, u32[]{:S(2)}) copy-start(bf16[8,2,2,128,128]{4,3,2,1,0:T(8,128)(2,1)} %param.11) | copy-start | bytes 3145732
  6.5 48.3 %copy-start.2 = (bf16[1,1,32,128,128]{4,3,2,1,0:T(8,128)(2,1)S(1)}, bf16[1,1,32,128,128]{4,3,2,1,0:T(8,128)(2,1)}, u32[]{:S(2)}) copy-start(bf16[1,1,32,128,128]{4,3,2,1,0:T(8,128)(2,1)} %param.14) | copy-start | bytes 3145732
  6.5 76.1 %all-gather.2.cloned.1.call-start = ((), (), s32[]{:S(2)}) async-start(), calls=%async_computation.1 | async-start | bytes 4718592 | tf_op jit(solution)/shard_map/all_gather | solution.py:253
  8.6 30.1 %collective-permute-start.12 = (bf16[32,128,128]{2,1,0:T(8,128)(2,1)}, bf16[32,128,128]{2,1,0:T(8,128)(2,1)S(1)}, u32[]{:S(2)}, u32[]{:S(2)}) collective-permute-start(bf16[32,128,128]{2,1,0:T(8,128)(2,1)} %bitcast.18), channel_id=1, source_target_pairs={{0,19},{2,17},{16,2},{18,0},{1,18},{3,16},{17,3},{19,1},{4,23},{6,... | collective-permute-start | bytes 3145736 | tf_op jit(solution)/shard_map/ppermute | solution.py:34
  12.8 25.9 %collective-permute-start.11 = (bf16[32,128,128]{2,1,0:T(8,128)(2,1)}, bf16[32,128,128]{2,1,0:T(8,128)(2,1)}, u32[]{:S(2)}, u32[]{:S(2)}) collective-permute-start(bf16[32,128,128]{2,1,0:T(8,128)(2,1)} %bitcast.19), channel_id=1, source_target_pairs={{0,2},{2,0},{1,3},{3,1},{4,6},{6,4},{5,7},{7,5},{8,10},{10,8},{9,1... | collective-permute-start | bytes 3145736 | tf_op jit(solution)/shard_map/ppermute | solution.py:44
  12.8 25.9 %collective-permute-start.10 = (bf16[32,128,128]{2,1,0:T(8,128)(2,1)}, bf16[32,128,128]{2,1,0:T(8,128)(2,1)}, u32[]{:S(2)}, u32[]{:S(2)}) collective-permute-start(bf16[32,128,128]{2,1,0:T(8,128)(2,1)} %bitcast.20), channel_id=1, source_target_pairs={{0,16},{2,18},{16,1},{18,3},{1,17},{3,19},{17,0},{19,2},{4,20},{6,... | collective-permute-start | bytes 3145736 | tf_op jit(solution)/shard_map/ppermute | solution.py:34
  17.8 20.9 %all-to-all-start = ((s32[64,1,128]{2,1,0:T(1,128)}), s32[64,1,128]{2,1,0:T(1,128)S(1)}, u32[]{:S(2)}, u32[]{:S(2)}) async-start(s32[64,1,128]{2,1,0:T(1,128)} %broadcast_in_dim.36), calls=%async_computation | async-start | bytes 65536 | tf_op jit(solution)/shard_map/all_to_all | solution.py:268
  29.3 6.8 %collective-permute-start.9 = (s32[2,32]{1,0:T(2,128)S(1)}, s32[2,32]{1,0:T(2,128)S(1)}, u32[]{:S(2)}, u32[]{:S(2)}) collective-permute-start(s32[2,32]{1,0:T(2,128)S(1)} %pad_add_fusion.own), channel_id=1, source_target_pairs={{0,19},{2,17},{16,2},{18,0},{1,18},{3,16},{17,3},{19,1},{4,23},{6,... | collective-permute-start | bytes 776 | tf_op jit(solution)/shard_map/ppermute | solution.py:34
  32.7 5.9 %collective-permute-start.8 = (s32[2,32]{1,0:T(2,128)S(1)}, s32[2,32]{1,0:T(2,128)S(1)}, u32[]{:S(2)}, u32[]{:S(2)}) collective-permute-start(s32[2,32]{1,0:T(2,128)S(1)} %pad_add_fusion.own), channel_id=1, source_target_pairs={{0,16},{2,18},{16,1},{18,3},{1,17},{3,19},{17,0},{19,2},{4,20},{6,... | collective-permute-start | bytes 776 | tf_op jit(solution)/shard_map/ppermute | solution.py:34
  38.7 15.1 %copy-start.3 = (bf16[32,128,128]{2,1,0:T(8,128)(2,1)}, bf16[32,128,128]{2,1,0:T(8,128)(2,1)S(1)}, u32[]{:S(2)}) copy-start(bf16[32,128,128]{2,1,0:T(8,128)(2,1)S(1)} %collective-permute-done.12.rest_3_) | copy-start | bytes 3145732
  42.3 19.4 %collective-permute-start.13 = (bf16[1040,128]{1,0:T(8,128)(2,1)S(1)}, bf16[1040,128]{1,0:T(8,128)(2,1)S(1)}, u32[]{:S(2)}, u32[]{:S(2)}) collective-permute-start(bf16[1040,128]{1,0:T(8,128)(2,1)S(1)} %get-tuple-element.93), channel_id=1, source_target_pairs={{0,128},{32,160},{64,192},{96,224},{128,0},{160,32},{192,64},{224,... | collective-permute-start | bytes 798728 | tf_op jit(solution)/shard_map/ppermute | solution.py:40
  49.4 32.6 %collective-permute-start.14 = (bf16[1040,128]{1,0:T(8,128)(2,1)S(1)}, bf16[1040,128]{1,0:T(8,128)(2,1)S(1)}, u32[]{:S(2)}, u32[]{:S(2)}) collective-permute-start(bf16[1040,128]{1,0:T(8,128)(2,1)S(1)} %get-tuple-element.94), channel_id=1, source_target_pairs={{0,96},{32,128},{64,160},{96,192},{128,224},{160,0},{192,32},{224,... | collective-permute-start | bytes 798728 | tf_op jit(solution)/shard_map/ppermute | solution.py:40
  51.3 31.3 %collective-permute-start.15 = (bf16[1040,128]{1,0:T(8,128)(2,1)S(1)}, bf16[1040,128]{1,0:T(8,128)(2,1)}, u32[]{:S(2)}, u32[]{:S(2)}) collective-permute-start(bf16[1040,128]{1,0:T(8,128)(2,1)S(1)} %get-tuple-element.95), channel_id=1, source_target_pairs={{0,160},{32,192},{64,224},{96,0},{128,32},{160,64},{192,96},{224,1... | collective-permute-start | bytes 798728 | tf_op jit(solution)/shard_map/ppermute | solution.py:40
  53.8 34.9 %collective-permute-start.16 = (bf16[1040,128]{1,0:T(8,128)(2,1)S(1)}, bf16[1040,128]{1,0:T(8,128)(2,1)}, u32[]{:S(2)}, u32[]{:S(2)}) collective-permute-start(bf16[1040,128]{1,0:T(8,128)(2,1)S(1)} %get-tuple-element.99), channel_id=1, source_target_pairs={{0,64},{32,96},{64,128},{96,160},{128,192},{160,224},{192,0},{224,... | collective-permute-start | bytes 798728 | tf_op jit(solution)/shard_map/ppermute | solution.py:40
  59.6 30.6 %collective-permute-start.17 = (bf16[1040,128]{1,0:T(8,128)(2,1)S(1)}, bf16[1040,128]{1,0:T(8,128)(2,1)}, u32[]{:S(2)}, u32[]{:S(2)}) collective-permute-start(bf16[1040,128]{1,0:T(8,128)(2,1)S(1)} %get-tuple-element.100), channel_id=1, source_target_pairs={{0,192},{32,224},{64,0},{96,32},{128,64},{160,96},{192,128},{224,1... | collective-permute-start | bytes 798728 | tf_op jit(solution)/shard_map/ppermute | solution.py:40
  61.7 20.2 %copy-start.6 = (bf16[1040,128]{1,0:T(8,128)(2,1)}, bf16[1040,128]{1,0:T(8,128)(2,1)S(1)}, u32[]{:S(2)}) copy-start(bf16[1040,128]{1,0:T(8,128)(2,1)S(1)} %collective-permute-done.13.rest_1_) | copy-start | bytes 798724
  61.7 33.8 %collective-permute-start.18 = (bf16[1040,128]{1,0:T(8,128)(2,1)S(1)}, bf16[1040,128]{1,0:T(8,128)(2,1)}, u32[]{:S(2)}, u32[]{:S(2)}) collective-permute-start(bf16[1040,128]{1,0:T(8,128)(2,1)S(1)} %get-tuple-element.101), channel_id=1, source_target_pairs={{0,32},{32,64},{64,96},{96,128},{128,160},{160,192},{192,224},{224... | collective-permute-start | bytes 798728 | tf_op jit(solution)/shard_map/ppermute | solution.py:40
  81.9 0.7 copy-start.8
  81.9 13.9 %collective-permute-start.19 = (bf16[1040,128]{1,0:T(8,128)(2,1)S(1)}, bf16[1040,128]{1,0:T(8,128)(2,1)}, u32[]{:S(2)}, u32[]{:S(2)}) collective-permute-start(bf16[1040,128]{1,0:T(8,128)(2,1)S(1)} %get-tuple-element.102), channel_id=1, source_target_pairs={{0,224},{32,0},{64,32},{96,64},{128,96},{160,128},{192,160},{224,1... | collective-permute-start | bytes 798728 | tf_op jit(solution)/shard_map/ppermute | solution.py:40
  82.6 13.2 %copy-start.1 = (bf16[8,16,128,128]{3,2,1,0:T(8,128)(2,1)S(1)}, bf16[8,16,128,128]{3,2,1,0:T(8,128)(2,1)}, u32[]{:S(2)}) copy-start(bf16[8,16,128,128]{3,2,1,0:T(8,128)(2,1)} %all-gather.2.cloned.1.call-done.a_all) | copy-start | bytes 12582916
  88.7 15.8 %copy-start.4 = (bf16[32,128,128]{2,1,0:T(8,128)(2,1)S(1)}, bf16[32,128,128]{2,1,0:T(8,128)(2,1)}, u32[]{:S(2)}) copy-start(bf16[32,128,128]{2,1,0:T(8,128)(2,1)} %copy-done.3) | copy-start | bytes 3145732
  88.7 15.8 %copy-start.5 = (bf16[2064,128]{1,0:T(8,128)(2,1)S(1)}, bf16[2064,128]{1,0:T(8,128)(2,1)}, u32[]{:S(2)}) copy-start(bf16[2064,128]{1,0:T(8,128)(2,1)} %get-tuple-element.92.rest_0_) | copy-start | bytes 1585156
  88.7 15.8 %copy-start.7 = (bf16[1040,128]{1,0:T(8,128)(2,1)S(1)}, bf16[1040,128]{1,0:T(8,128)(2,1)}, u32[]{:S(2)}) copy-start(bf16[1040,128]{1,0:T(8,128)(2,1)} %copy-done.6) | copy-start | bytes 798724
  88.7 15.8 %copy-start.9 = (bf16[1040,128]{1,0:T(8,128)(2,1)S(1)}, bf16[1040,128]{1,0:T(8,128)(2,1)}, u32[]{:S(2)}) copy-start(bf16[1040,128]{1,0:T(8,128)(2,1)} %copy-done.8) | copy-start | bytes 798724
  100.6 3.9 %collective-permute-start.20 = (f32[16,128,128]{2,1,0:T(8,128)S(1)}, f32[16,128,128]{2,1,0:T(8,128)S(1)}, u32[]{:S(2)}, u32[]{:S(2)}) collective-permute-start(f32[16,128,128]{2,1,0:T(8,128)S(1)} %get-tuple-element.105), channel_id=1, source_target_pairs={{0,2},{2,0},{1,3},{3,1},{4,6},{6,4},{5,7},{7,5},{8,10},{10,8},{9,1... | collective-permute-start | bytes 3145736 | tf_op jit(solution)/shard_map/ppermute | solution.py:44
  104.6 0.8 copy-start.10
Sparse Core Ops, SparseCore 0:
  9.2 39.1 all-gather.1
where the time goes:
time: 113 us; the launch traced here: 112 us
  starting transfers between devices  36.8 us (33%)
  waiting for transfers between devices  33.5 us (30%)
  Pallas kernels  18.9 us (17%)
  between operations  14.8 us (13%)
  local copies, waits for them, and re-layouts  5.24 us (5%)
  other arithmetic  2.91 us (3%)
    ppermute x7, waiting for transfers between devices, shift_z(): return lax.ppermute(value, 'z', [(z, (z + steps) % NZ) for z in range(NZ)])  26.4 us
    ppermute x7, starting transfers between devices, shift_z(): return lax.ppermute(value, 'z', [(z, (z + steps) % NZ) for z in range(NZ)])  15.6 us
    all_to_all x1, starting transfers between devices, body(): lax.all_to_all(meta, ('z', 'x', 'core'), 0, 0)  11.5 us
    pallas_call x2, Pallas kernels, consume(): pl.pallas_call(functools.partial(consume_kernel, shifts, parts), out_shap...  10.6 us
    pallas_call x2, Pallas kernels, pack(): pl.pallas_call(functools.partial(pack_kernel, shifts, lo, size), out_shap...  8.27 us
    ppermute x4, starting transfers between devices, along_y(): return lax.ppermute(value, ('yl', 'core', 'rep'), pairs)  8.04 us
    ppermute x4, waiting for transfers between devices, along_y(): return lax.ppermute(value, ('yl', 'core', 'rep'), pairs)  5.87 us
    unnamed x22, local copies, waits for them, and re-layouts  2.73 us
  transfers between devices with their start and end apart: 15, of which 8 were waited for; matrix products, arithmetic and copies ran while one was open for 4% of the time, Pallas kernels for 13%

commit v1 on v0

--- a/solution.py
+++ b/solution.py
@@ -18,6 +18,7 @@
 HDR = 16
 LANES = 128
 SHIFTS = (0, 4, 3, -3, 2, -2, 1, -1)
+WIDE = 256
 FAR = 5
 EARLY = 4
 
@@ -83,10 +84,13 @@
         return jnp.where(first_half, low, pltpu.roll(rows, LANES - start - length, 1))
 
     wanted = jnp.where(lane < PAIR, pick(me, 0, PAIR), -2)
-    twin_meta = meta[me, pl.ds(x * NCORE + 1 - core, 1), :]
-    twin_own = {
-        (n, m): twin_meta[:, 4 * PAIR + n * MB + m : 4 * PAIR + n * MB + m + 1] for n in range(2) for m in range(MB)
-    }
+    def as_list(row, start):
+        return {
+            (n, m): row[:, start + n * MB + m : start + n * MB + m + 1] for n in range(2) for m in range(MB)
+        }
+
+    twin_own = as_list(meta[me, pl.ds(x * NCORE + 1 - core, 1), :], 4 * PAIR)
+    other, twin_other = as_list(other[0:1, :], 0), as_list(twin_other[0:1, :], 0)
     code = find_codes(wanted, pick(x * NCORE + core, 2 * PAIR, ROWS * SC), own, other, is_own, lane)
     twin = find_codes(wanted, pick(x * NCORE + 1 - core, 2 * PAIR, ROWS * SC), twin_own, twin_other, is_own, lane)
     code, twin = jnp.where(core == 0, code, twin), jnp.where(core == 0, twin, code)
@@ -149,7 +153,7 @@
             jax.ShapeDtypeStruct(((size if shift else PAIR) * BS + HDR, BS), jnp.bfloat16)
             for shift in shifts
         ],
-        in_specs=[vmem] + [smem] * 3 + [hbm] * 4,
+        in_specs=[vmem, smem, vmem, vmem] + [hbm] * 4,
         out_specs=[vmem] * len(shifts),
         scratch_shapes=[
             pltpu.VMEM((4 * MB, BS, BS), jnp.bfloat16),
@@ -261,7 +265,8 @@
     b_own = b_blocks[0, 0]
 
     blocks = [b_own, along_y(b_own, 1, 0), swap(b_own), along_y(b_own, -1, 1)]
-    lists = [own, along_y(own, 1, 0), along_y(own, -1, 1)]
+    wide = jnp.broadcast_to(jnp.pad(own.reshape(1, 2 * MB), ((0, 0), (0, LANES - 2 * MB))), (WIDE, LANES))
+    lists = [own, along_y(wide, 1, 0), along_y(wide, -1, 1)]
 
     meta = jnp.concatenate([a_meta.reshape(2 * PAIR), c_meta.reshape(2 * ROWS * SC), own.reshape(2 * MB)])
     meta = jnp.broadcast_to(meta[None, :], (NZ * NX * NCORE, LANES))

time: 113 us -> 116 us (1.027)
  blocking collectives: 0 us -> 20.8 us
  starting transfers between devices: 36.8 us -> 23.6 us
  waiting for transfers between devices: 33.5 us -> 27.5 us
  local copies, waits for them, and re-layouts: 5.24 us -> 6.43 us
    all_to_all x0 -> x1, blocking collectives: none -> 20.8 us  [body(): lax.all_to_all(meta, ('z', 'x', 'core'), 0, 0)]
    all_to_all x1 -> x0, starting transfers between devices: 11.5 us -> none  [body(): lax.all_to_all(meta, ('z', 'x', 'core'), 0, 0)]
    ppermute x4, waiting for transfers between devices: 5.87 us -> 0.01 us  [along_y(): return lax.ppermute(value, ('yl', 'core', 'rep'), pairs)]
    unnamed x22 -> x32, local copies, waits for them, and re-layouts: 2.73 us -> 3.37 us
  transfers between devices with their start and end apart: 15 -> 14, of which waited for: 8 -> 5; matrix products, arithmetic and copies ran while one was open for 4% -> 5% of each run, Pallas kernels for 13% -> 13%
where the time goes in v1:
time: 116 us
  waiting for transfers between devices  27.5 us (24%)
  starting transfers between devices  23.6 us (20%)
  blocking collectives  20.8 us (18%)
  Pallas kernels  19.3 us (17%)
  between operations  14.9 us (13%)
  local copies, waits for them, and re-layouts  6.43 us (6%)
  other arithmetic  3.58 us (3%)
    ppermute x7, waiting for transfers between devices, shift_z(): return lax.ppermute(value, 'z', [(z, (z + steps) % NZ) for z in range(NZ)])  26.3 us
    all_to_all x1, blocking collectives, body(): lax.all_to_all(meta, ('z', 'x', 'core'), 0, 0)  20.8 us
    ppermute x7, starting transfers between devices, shift_z(): return lax.ppermute(value, 'z', [(z, (z + steps) % NZ) for z in range(NZ)])  14.6 us
    pallas_call x2, Pallas kernels, consume(): pl.pallas_call(functools.partial(consume_kernel, shifts, parts), out_shap...  10.3 us
    pallas_call x2, Pallas kernels, pack(): pl.pallas_call(functools.partial(pack_kernel, shifts, lo, size), out_shap...  8.98 us
    ppermute x4, starting transfers between devices, along_y(): return lax.ppermute(value, ('yl', 'core', 'rep'), pairs)  7.63 us
    unnamed x32, local copies, waits for them, and re-layouts  3.37 us
  transfers between devices with their start and end apart: 14, of which 5 were waited for; matrix products, arithmetic and copies ran while one was open for 5% of the time, Pallas kernels for 13%

profile of v1, /device:TPU:1, one launch (start us, length us, event | category | flops | bytes accessed | tf_op | source)
XLA Modules:
  0.0 116.1 jit_solution(1048587963803935730)
XLA Ops:
  6.5 1.2 %copy-done = bf16[8,2,2,128,128]{4,3,2,1,0:T(8,128)(2,1)S(1)} copy-done((bf16[8,2,2,128,128]{4,3,2,1,0:T(8,128)(2,1)S(1)}, bf16[8,2,2,128,128]{4,3,2,1,0:T(8,128)(2,1)}, u32[]{:S(2)}) %copy-start) | copy-done | bytes 1048600
  7.8 0.8 constant_dynamic-slice_fusion
  8.6 0.0 all-gather.2.cloned.1.call-update
  8.6 4.2 %collective-permute-start.12 = (bf16[32,128,128]{2,1,0:T(8,128)(2,1)}, bf16[32,128,128]{2,1,0:T(8,128)(2,1)S(1)}, u32[]{:S(2)}, u32[]{:S(2)}) collective-permute-start(bf16[32,128,128]{2,1,0:T(8,128)(2,1)} %bitcast.20), channel_id=1, source_target_pairs={{0,19},{2,17},{16,2},{18,0},{1,18},{3,16},{17,3},{19,1},{4,23},{6,... | collective-permute-start | bytes 3145736 | tf_op jit(solution)/shard_map/ppermute | solution.py:35
  12.8 0.5 collective-permute-start.10
  14.0 0.7 compare_select_fusion.1
  14.6 0.7 pad_add_fusion.own
  15.3 0.1 reshape.93
  15.4 3.0 %collective-permute-start.9 = (s32[256,128]{1,0:T(8,128)S(1)}, s32[256,128]{1,0:T(8,128)S(1)}, u32[]{:S(2)}, u32[]{:S(2)}) collective-permute-start(s32[256,128]{1,0:T(8,128)S(1)} %broadcast_in_dim.45), channel_id=1, source_target_pairs={{0,19},{2,17},{16,2},{18,0},{1,18},{3,16},{17,3},{19,1},{4,23},{6,... | collective-permute-start | bytes 393224 | tf_op jit(solution)/shard_map/ppermute | solution.py:35
  18.3 0.0 collective-permute-start.8
  18.3 0.6 reshape.91
  19.0 0.7 fusion
  19.7 0.1 copy.19
  19.7 0.6 reshape.90
  20.3 0.7 compare_select_fusion
  21.0 0.1 copy.18
  21.1 0.1 reshape.89
  21.2 0.7 pad_add_fusion.1
  22.0 20.8 %all_to_all.6 = s32[64,1,128]{2,1,0:T(1,128)S(1)} all-to-all(s32[64,1,128]{2,1,0:T(1,128)S(1)} %broadcast_in_dim.43), channel_id=1, replica_groups=mesh['z'=8,'yl'=2,'x'=4,'core'=2,'rep'=2] {'z','x','core'}, dimensions={0} | all-to-all | bytes 65536 | tf_op jit(solution)/shard_map/all_to_all | solution.py:273
  42.7 0.0 collective-permute-done.9.twin_other
  42.8 0.0 collective-permute-done.8.other
  42.8 0.0 collective-permute-done.10.rest_1_
  42.8 0.6 copy-done.6
  43.4 4.1 %pack.5 = (bf16[1040,128]{1,0:T(8,128)(2,1)S(1)}, bf16[1040,128]{1,0:T(8,128)(2,1)S(1)}, bf16[1040,128]{1,0:T(8,128)(2,1)S(1)}, bf16[1040,128]{1,0:T(8,128)(2,1)S(1)}) custom-call(s32[8,8,128]{2,1,0:T(8,128)S(1)} %bitcast.27, s32[2,32]{1,0:T(2,128)S(1)} %pad_add_fusion.own, s32[256,128]{1,0:T(8,128)} %copy-done.6, ...), custom_call_target="tpu_custom_call" | custom-call | tf_op jit(solution)/shard_map/pack/pallas_call | solution.py:150
  47.5 5.6 %collective-permute-start.13 = (bf16[1040,128]{1,0:T(8,128)(2,1)S(1)}, bf16[1040,128]{1,0:T(8,128)(2,1)S(1)}, u32[]{:S(2)}, u32[]{:S(2)}) collective-permute-start(bf16[1040,128]{1,0:T(8,128)(2,1)S(1)} %get-tuple-element.93), channel_id=1, source_target_pairs={{0,128},{32,160},{64,192},{96,224},{128,0},{160,32},{192,64},{224,... | collective-permute-start | bytes 798728 | tf_op jit(solution)/shard_map/ppermute | solution.py:41
  53.1 1.7 %collective-permute-start.14 = (bf16[1040,128]{1,0:T(8,128)(2,1)S(1)}, bf16[1040,128]{1,0:T(8,128)(2,1)S(1)}, u32[]{:S(2)}, u32[]{:S(2)}) collective-permute-start(bf16[1040,128]{1,0:T(8,128)(2,1)S(1)} %get-tuple-element.94), channel_id=1, source_target_pairs={{0,96},{32,128},{64,160},{96,192},{128,224},{160,0},{192,32},{224,... | collective-permute-start | bytes 798728 | tf_op jit(solution)/shard_map/ppermute | solution.py:41
  54.7 2.8 %collective-permute-start.15 = (bf16[1040,128]{1,0:T(8,128)(2,1)S(1)}, bf16[1040,128]{1,0:T(8,128)(2,1)}, u32[]{:S(2)}, u32[]{:S(2)}) collective-permute-start(bf16[1040,128]{1,0:T(8,128)(2,1)S(1)} %get-tuple-element.95), channel_id=1, source_target_pairs={{0,160},{32,192},{64,224},{96,0},{128,32},{160,64},{192,96},{224,1... | collective-permute-start | bytes 798728 | tf_op jit(solution)/shard_map/ppermute | solution.py:41
  57.6 1.2 %collective-permute-start.16 = (bf16[1040,128]{1,0:T(8,128)(2,1)S(1)}, bf16[1040,128]{1,0:T(8,128)(2,1)}, u32[]{:S(2)}, u32[]{:S(2)}) collective-permute-start(bf16[1040,128]{1,0:T(8,128)(2,1)S(1)} %get-tuple-element.99), channel_id=1, source_target_pairs={{0,64},{32,96},{64,128},{96,160},{128,192},{160,224},{192,0},{224,... | collective-permute-start | bytes 798728 | tf_op jit(solution)/shard_map/ppermute | solution.py:41
  58.8 4.9 %pack.4 = (bf16[1040,128]{1,0:T(8,128)(2,1)S(1)}, bf16[1040,128]{1,0:T(8,128)(2,1)S(1)}, bf16[1040,128]{1,0:T(8,128)(2,1)S(1)}, bf16[2064,128]{1,0:T(8,128)(2,1)}) custom-call(s32[8,8,128]{2,1,0:T(8,128)S(1)} %bitcast.28, s32[2,32]{1,0:T(2,128)S(1)} %pad_add_fusion.own, s32[256,128]{1,0:T(8,128)S(1)} %copy-done.7, ...), custom_call_target="tpu_custom_call" | custom-call | tf_op jit(solution)/shard_map/pack/pallas_call | solution.py:150
  63.7 1.9 %collective-permute-start.17 = (bf16[1040,128]{1,0:T(8,128)(2,1)S(1)}, bf16[1040,128]{1,0:T(8,128)(2,1)}, u32[]{:S(2)}, u32[]{:S(2)}) collective-permute-start(bf16[1040,128]{1,0:T(8,128)(2,1)S(1)} %get-tuple-element.100), channel_id=1, source_target_pairs={{0,192},{32,224},{64,0},{96,32},{128,64},{160,96},{192,128},{224,1... | collective-permute-start | bytes 798728 | tf_op jit(solution)/shard_map/ppermute | solution.py:41
  65.5 0.0 collective-permute-done.13.rest_1_
  65.5 1.5 %collective-permute-start.18 = (bf16[1040,128]{1,0:T(8,128)(2,1)S(1)}, bf16[1040,128]{1,0:T(8,128)(2,1)}, u32[]{:S(2)}, u32[]{:S(2)}) collective-permute-start(bf16[1040,128]{1,0:T(8,128)(2,1)S(1)} %get-tuple-element.101), channel_id=1, source_target_pairs={{0,32},{32,64},{64,96},{96,128},{128,160},{160,192},{192,224},{224... | collective-permute-start | bytes 798728 | tf_op jit(solution)/shard_map/ppermute | solution.py:41
  67.0 19.2 %collective-permute-done.14.rest_2_ = bf16[1040,128]{1,0:T(8,128)(2,1)S(1)} collective-permute-done((bf16[1040,128]{1,0:T(8,128)(2,1)S(1)}, bf16[1040,128]{1,0:T(8,128)(2,1)S(1)}, u32[]{:S(2)}, u32[]{:S(2)}) %collective-permute-start.14) | collective-permute-done | bytes 266272 | tf_op jit(solution)/shard_map/ppermute | solution.py:41
  86.2 0.0 collective-permute-start.19
  86.3 0.7 copy-done.11
  87.0 0.1 broadcast_in_dim.38.own_in.twin_in
  87.1 5.7 %consume.4 = (f32[16,128,128]{2,1,0:T(8,128)S(1)}, f32[16,128,128]{2,1,0:T(8,128)S(1)}, s32[8,128]{1,0:T(8,128)S(1)}) custom-call(bf16[8,16,128,128]{3,2,1,0:T(8,128)(2,1)} %all-gather.2.cloned.1.call-done.a_all, f32[16,128,128]{2,1,0:T(8,128)S(1)} %broadcast_in_dim.38.own_in.twin_in, f32[16,128,128]{2,1,0:T(8,128)S(1)} %broadcast_in_dim.38.own_in.twin_in, ...), custom_call_target="tpu_custom_call" | custom-call | flops 167772160 | bytes 8388608 | tf_op jit(solution)/shard_map/consume/pallas_call | solution.py:233
  92.9 1.5 %collective-permute-done.17.rest_1_ = bf16[1040,128]{1,0:T(8,128)(2,1)} collective-permute-done((bf16[1040,128]{1,0:T(8,128)(2,1)S(1)}, bf16[1040,128]{1,0:T(8,128)(2,1)}, u32[]{:S(2)}, u32[]{:S(2)}) %collective-permute-start.17) | collective-permute-done | bytes 266272 | tf_op jit(solution)/shard_map/ppermute | solution.py:41
  94.4 5.0 %collective-permute-done.18.rest_2_ = bf16[1040,128]{1,0:T(8,128)(2,1)} collective-permute-done((bf16[1040,128]{1,0:T(8,128)(2,1)S(1)}, bf16[1040,128]{1,0:T(8,128)(2,1)}, u32[]{:S(2)}, u32[]{:S(2)}) %collective-permute-start.18) | collective-permute-done | bytes 266272 | tf_op jit(solution)/shard_map/ppermute | solution.py:41
  99.4 0.6 collective-permute-done.19.rest_3_
  100.0 4.6 %consume.5 = (f32[16,128,128]{2,1,0:T(8,128)S(1)}, f32[16,128,128]{2,1,0:T(8,128)S(1)}, s32[8,128]{1,0:T(8,128)S(1)}) custom-call(bf16[8,16,128,128]{3,2,1,0:T(8,128)(2,1)S(1)} %copy-done.1, f32[16,128,128]{2,1,0:T(8,128)S(1)} %get-tuple-element.96.own_in, f32[16,128,128]{2,1,0:T(8,128)S(1)} %get-tuple-element.97.twin_in, ...), custom_call_target="tpu_custom_call" | custom-call | flops 167772160 | bytes 8388608 | tf_op jit(solution)/shard_map/consume/pallas_call | solution.py:233
  104.6 1.4 %collective-permute-start.20 = (f32[16,128,128]{2,1,0:T(8,128)S(1)}, f32[16,128,128]{2,1,0:T(8,128)S(1)}, u32[]{:S(2)}, u32[]{:S(2)}) collective-permute-start(f32[16,128,128]{2,1,0:T(8,128)S(1)} %get-tuple-element.105), channel_id=1, source_target_pairs={{0,2},{2,0},{1,3},{3,1},{4,6},{6,4},{5,7},{7,5},{8,10},{10,8},{9,1... | collective-permute-start | bytes 3145736 | tf_op jit(solution)/shard_map/ppermute | solution.py:45
  106.0 0.5 slice.3
  107.1 1.1 collective-permute-done.20
  108.3 0.2 conditional.1
  108.3 0.2 add_convert_fusion
  108.5 0.0 copy-start.15
  108.5 0.8 copy-done.15
  (38 shorter events, 0.1 us)
Async XLA Ops:
  6.5 1.2 %copy-start = (bf16[8,2,2,128,128]{4,3,2,1,0:T(8,128)(2,1)S(1)}, bf16[8,2,2,128,128]{4,3,2,1,0:T(8,128)(2,1)}, u32[]{:S(2)}) copy-start(bf16[8,2,2,128,128]{4,3,2,1,0:T(8,128)(2,1)} %param.11) | copy-start | bytes 3145732
  6.5 52.2 %copy-start.2 = (bf16[1,1,32,128,128]{4,3,2,1,0:T(8,128)(2,1)S(1)}, bf16[1,1,32,128,128]{4,3,2,1,0:T(8,128)(2,1)}, u32[]{:S(2)}) copy-start(bf16[1,1,32,128,128]{4,3,2,1,0:T(8,128)(2,1)} %param.14) | copy-start | bytes 3145732
  6.5 80.4 %all-gather.2.cloned.1.call-start = ((), (), s32[]{:S(2)}) async-start(), calls=%async_computation.1 | async-start | bytes 4718592 | tf_op jit(solution)/shard_map/all_gather | solution.py:257
  8.6 34.1 %collective-permute-start.12 = (bf16[32,128,128]{2,1,0:T(8,128)(2,1)}, bf16[32,128,128]{2,1,0:T(8,128)(2,1)S(1)}, u32[]{:S(2)}, u32[]{:S(2)}) collective-permute-start(bf16[32,128,128]{2,1,0:T(8,128)(2,1)} %bitcast.20), channel_id=1, source_target_pairs={{0,19},{2,17},{16,2},{18,0},{1,18},{3,16},{17,3},{19,1},{4,23},{6,... | collective-permute-start | bytes 3145736 | tf_op jit(solution)/shard_map/ppermute | solution.py:35
  12.8 30.0 %collective-permute-start.11 = (bf16[32,128,128]{2,1,0:T(8,128)(2,1)}, bf16[32,128,128]{2,1,0:T(8,128)(2,1)}, u32[]{:S(2)}, u32[]{:S(2)}) collective-permute-start(bf16[32,128,128]{2,1,0:T(8,128)(2,1)} %bitcast.21), channel_id=1, source_target_pairs={{0,2},{2,0},{1,3},{3,1},{4,6},{6,4},{5,7},{7,5},{8,10},{10,8},{9,1... | collective-permute-start | bytes 3145736 | tf_op jit(solution)/shard_map/ppermute | solution.py:45
  12.8 30.0 %collective-permute-start.10 = (bf16[32,128,128]{2,1,0:T(8,128)(2,1)}, bf16[32,128,128]{2,1,0:T(8,128)(2,1)}, u32[]{:S(2)}, u32[]{:S(2)}) collective-permute-start(bf16[32,128,128]{2,1,0:T(8,128)(2,1)} %bitcast.22), channel_id=1, source_target_pairs={{0,16},{2,18},{16,1},{18,3},{1,17},{3,19},{17,0},{19,2},{4,20},{6,... | collective-permute-start | bytes 3145736 | tf_op jit(solution)/shard_map/ppermute | solution.py:35
  15.4 27.4 %collective-permute-start.9 = (s32[256,128]{1,0:T(8,128)S(1)}, s32[256,128]{1,0:T(8,128)S(1)}, u32[]{:S(2)}, u32[]{:S(2)}) collective-permute-start(s32[256,128]{1,0:T(8,128)S(1)} %broadcast_in_dim.45), channel_id=1, source_target_pairs={{0,19},{2,17},{16,2},{18,0},{1,18},{3,16},{17,3},{19,1},{4,23},{6,... | collective-permute-start | bytes 393224 | tf_op jit(solution)/shard_map/ppermute | solution.py:35
  18.3 24.4 %collective-permute-start.8 = (s32[256,128]{1,0:T(8,128)S(1)}, s32[256,128]{1,0:T(8,128)S(1)}, u32[]{:S(2)}, u32[]{:S(2)}) collective-permute-start(s32[256,128]{1,0:T(8,128)S(1)} %broadcast_in_dim.45), channel_id=1, source_target_pairs={{0,16},{2,18},{16,1},{18,3},{1,17},{3,19},{17,0},{19,2},{4,20},{6,... | collective-permute-start | bytes 393224 | tf_op jit(solution)/shard_map/ppermute | solution.py:35
  42.7 43.5 %copy-start.13 = (s32[64,1,128]{2,1,0:T(1,128)}, s32[64,1,128]{2,1,0:T(1,128)S(1)}, u32[]{:S(2)}) copy-start(s32[64,1,128]{2,1,0:T(1,128)S(1)} %all_to_all.6) | copy-start | bytes 98308
  42.8 0.7 copy-start.6
  42.8 14.8 %copy-start.3 = (bf16[32,128,128]{2,1,0:T(8,128)(2,1)}, bf16[32,128,128]{2,1,0:T(8,128)(2,1)S(1)}, u32[]{:S(2)}) copy-start(bf16[32,128,128]{2,1,0:T(8,128)(2,1)S(1)} %collective-permute-done.12.rest_3_) | copy-start | bytes 3145732
  43.4 15.3 %copy-start.7 = (s32[256,128]{1,0:T(8,128)S(1)}, s32[256,128]{1,0:T(8,128)}, u32[]{:S(2)}) copy-start(s32[256,128]{1,0:T(8,128)} %copy-done.6) | copy-start | bytes 393220
  47.5 18.0 %collective-permute-start.13 = (bf16[1040,128]{1,0:T(8,128)(2,1)S(1)}, bf16[1040,128]{1,0:T(8,128)(2,1)S(1)}, u32[]{:S(2)}, u32[]{:S(2)}) collective-permute-start(bf16[1040,128]{1,0:T(8,128)(2,1)S(1)} %get-tuple-element.93), channel_id=1, source_target_pairs={{0,128},{32,160},{64,192},{96,224},{128,0},{160,32},{192,64},{224,... | collective-permute-start | bytes 798728 | tf_op jit(solution)/shard_map/ppermute | solution.py:41
  53.1 33.2 %collective-permute-start.14 = (bf16[1040,128]{1,0:T(8,128)(2,1)S(1)}, bf16[1040,128]{1,0:T(8,128)(2,1)S(1)}, u32[]{:S(2)}, u32[]{:S(2)}) collective-permute-start(bf16[1040,128]{1,0:T(8,128)(2,1)S(1)} %get-tuple-element.94), channel_id=1, source_target_pairs={{0,96},{32,128},{64,160},{96,192},{128,224},{160,0},{192,32},{224,... | collective-permute-start | bytes 798728 | tf_op jit(solution)/shard_map/ppermute | solution.py:41
  54.7 32.2 %collective-permute-start.15 = (bf16[1040,128]{1,0:T(8,128)(2,1)S(1)}, bf16[1040,128]{1,0:T(8,128)(2,1)}, u32[]{:S(2)}, u32[]{:S(2)}) collective-permute-start(bf16[1040,128]{1,0:T(8,128)(2,1)S(1)} %get-tuple-element.95), channel_id=1, source_target_pairs={{0,160},{32,192},{64,224},{96,0},{128,32},{160,64},{192,96},{224,1... | collective-permute-start | bytes 798728 | tf_op jit(solution)/shard_map/ppermute | solution.py:41
  57.6 35.3 %collective-permute-start.16 = (bf16[1040,128]{1,0:T(8,128)(2,1)S(1)}, bf16[1040,128]{1,0:T(8,128)(2,1)}, u32[]{:S(2)}, u32[]{:S(2)}) collective-permute-start(bf16[1040,128]{1,0:T(8,128)(2,1)S(1)} %get-tuple-element.99), channel_id=1, source_target_pairs={{0,64},{32,96},{64,128},{96,160},{128,192},{160,224},{192,0},{224,... | collective-permute-start | bytes 798728 | tf_op jit(solution)/shard_map/ppermute | solution.py:41
  63.7 30.7 %collective-permute-start.17 = (bf16[1040,128]{1,0:T(8,128)(2,1)S(1)}, bf16[1040,128]{1,0:T(8,128)(2,1)}, u32[]{:S(2)}, u32[]{:S(2)}) collective-permute-start(bf16[1040,128]{1,0:T(8,128)(2,1)S(1)} %get-tuple-element.100), channel_id=1, source_target_pairs={{0,192},{32,224},{64,0},{96,32},{128,64},{160,96},{192,128},{224,1... | collective-permute-start | bytes 798728 | tf_op jit(solution)/shard_map/ppermute | solution.py:41
  65.5 20.7 %copy-start.9 = (bf16[1040,128]{1,0:T(8,128)(2,1)}, bf16[1040,128]{1,0:T(8,128)(2,1)S(1)}, u32[]{:S(2)}) copy-start(bf16[1040,128]{1,0:T(8,128)(2,1)S(1)} %collective-permute-done.13.rest_1_) | copy-start | bytes 798724
  65.5 33.8 %collective-permute-start.18 = (bf16[1040,128]{1,0:T(8,128)(2,1)S(1)}, bf16[1040,128]{1,0:T(8,128)(2,1)}, u32[]{:S(2)}, u32[]{:S(2)}) collective-permute-start(bf16[1040,128]{1,0:T(8,128)(2,1)S(1)} %get-tuple-element.101), channel_id=1, source_target_pairs={{0,32},{32,64},{64,96},{96,128},{128,160},{160,192},{192,224},{224... | collective-permute-start | bytes 798728 | tf_op jit(solution)/shard_map/ppermute | solution.py:41
  86.2 0.7 copy-start.11
  86.2 13.8 %collective-permute-start.19 = (bf16[1040,128]{1,0:T(8,128)(2,1)S(1)}, bf16[1040,128]{1,0:T(8,128)(2,1)}, u32[]{:S(2)}, u32[]{:S(2)}) collective-permute-start(bf16[1040,128]{1,0:T(8,128)(2,1)S(1)} %get-tuple-element.102), channel_id=1, source_target_pairs={{0,224},{32,0},{64,32},{96,64},{128,96},{160,128},{192,160},{224,1... | collective-permute-start | bytes 798728 | tf_op jit(solution)/shard_map/ppermute | solution.py:41
  87.0 13.0 %copy-start.1 = (bf16[8,16,128,128]{3,2,1,0:T(8,128)(2,1)S(1)}, bf16[8,16,128,128]{3,2,1,0:T(8,128)(2,1)}, u32[]{:S(2)}) copy-start(bf16[8,16,128,128]{3,2,1,0:T(8,128)(2,1)} %all-gather.2.cloned.1.call-done.a_all) | copy-start | bytes 12582916
  92.8 15.5 %copy-start.4 = (bf16[32,128,128]{2,1,0:T(8,128)(2,1)S(1)}, bf16[32,128,128]{2,1,0:T(8,128)(2,1)}, u32[]{:S(2)}) copy-start(bf16[32,128,128]{2,1,0:T(8,128)(2,1)} %copy-done.3) | copy-start | bytes 3145732
  92.8 15.5 %copy-start.5 = (bf16[2064,128]{1,0:T(8,128)(2,1)S(1)}, bf16[2064,128]{1,0:T(8,128)(2,1)}, u32[]{:S(2)}) copy-start(bf16[2064,128]{1,0:T(8,128)(2,1)} %get-tuple-element.92.rest_0_) | copy-start | bytes 1585156
  92.8 15.5 %copy-start.8 = (s32[256,128]{1,0:T(8,128)S(1)}, s32[256,128]{1,0:T(8,128)}, u32[]{:S(2)}) copy-start(s32[256,128]{1,0:T(8,128)} %copy-done.6) | copy-start | bytes 393220
  92.8 15.4 %copy-start.10 = (bf16[1040,128]{1,0:T(8,128)(2,1)S(1)}, bf16[1040,128]{1,0:T(8,128)(2,1)}, u32[]{:S(2)}) copy-start(bf16[1040,128]{1,0:T(8,128)(2,1)} %copy-done.9) | copy-start | bytes 798724
  92.8 15.4 %copy-start.12 = (bf16[1040,128]{1,0:T(8,128)(2,1)S(1)}, bf16[1040,128]{1,0:T(8,128)(2,1)}, u32[]{:S(2)}) copy-start(bf16[1040,128]{1,0:T(8,128)(2,1)} %copy-done.11) | copy-start | bytes 798724
  92.8 15.4 %copy-start.14 = (s32[64,1,128]{2,1,0:T(1,128)S(1)}, s32[64,1,128]{2,1,0:T(1,128)}, u32[]{:S(2)}) copy-start(s32[64,1,128]{2,1,0:T(1,128)} %copy-done.13) | copy-start | bytes 98308
  104.6 3.7 %collective-permute-start.20 = (f32[16,128,128]{2,1,0:T(8,128)S(1)}, f32[16,128,128]{2,1,0:T(8,128)S(1)}, u32[]{:S(2)}, u32[]{:S(2)}) collective-permute-start(f32[16,128,128]{2,1,0:T(8,128)S(1)} %get-tuple-element.105), channel_id=1, source_target_pairs={{0,2},{2,0},{1,3},{3,1},{4,6},{6,4},{5,7},{7,5},{8,10},{10,8},{9,1... | collective-permute-start | bytes 3145736 | tf_op jit(solution)/shard_map/ppermute | solution.py:45
  108.5 0.8 copy-start.15
Sparse Core Ops, SparseCore 0:
  9.2 39.1 all-gather.1
